TPU v7x, 512 devices: a whole 4x8x8 slice. The times are simulated.
512 devices in a mesh: seq: 32 (over x, y), ch: 16 (over z, core).
Axes of the slice: x: 4, y: 8, z: 8, core: 2. Of those that a mesh axis runs over, the one named last changes fastest.
Arguments:
- first_gate: bfloat16 [8192, 4096], P('seq', 'ch'), parts along dimension 1, may hold values from -6 to 6
- second_gate: bfloat16 [8192, 4096], P('seq', 'ch'), parts along dimension 1, may hold values from -6 to 6
- values_in: bfloat16 [8192, 4096], P('seq', 'ch'), parts along dimension 1, may hold values from -6 to 6
- cotangent: bfloat16 [8192, 4096], P('seq', 'ch'), parts along dimension 1, may hold values from -6 to 6
- filters: bfloat16 [131072], P(('ch', 'seq')), parts along dimension 0, may hold values from -0.0625 to 0.0625
- skip_gain: float32 [4096], P('ch'), parts along dimension 0, may hold values from -4 to 4
Outputs:
- output: bfloat16 [8192, 4096], P('seq', 'ch'), parts along dimension 1
- grad_first: bfloat16 [8192, 4096], P('seq', 'ch'), parts along dimension 1
- grad_second: bfloat16 [8192, 4096], P('seq', 'ch'), parts along dimension 1
- grad_values: bfloat16 [8192, 4096], P('seq', 'ch'), parts along dimension 1
There are 16 independent parts, one for each index of `ch`. A program takes and returns all parts, laid end to end along the dimension named above; each array names one. Nothing has to cross between parts.
All inputs are finite; a program needn't handle non-finite values.
Results may differ from a plain program's by a relative error of at most 0.0049.
Values may be sent and summed in bfloat16 or wider, within the bound.
A program may use at most 64 MiB of HBM per device.

v0:
```python
import jax
import jax.numpy as jnp
from jax import lax
from jax.sharding import PartitionSpec as P


def on_device(first_gate, second_gate, values_in, cotangent, filters, skip_gain):
    shard_rows, channels = first_gate.shape
    block_rows = shard_rows // 2
    members = lax.axis_size("seq")
    position = lax.axis_index("seq")
    filter_taps = lax.all_gather(filters, "seq", axis=0, tiled=True)
    padded = jnp.concatenate([jnp.zeros((block_rows,), filter_taps.dtype), filter_taps])

    def lag_matrix(offset_blocks):
        window = lax.dynamic_slice_in_dim(padded, offset_blocks * block_rows, 2 * block_rows)
        reversed_taps = window[::-1]
        tiled = jnp.broadcast_to(reversed_taps, (block_rows, 2 * block_rows)).reshape(-1)
        skewed = tiled[: block_rows * (2 * block_rows - 1)].reshape(block_rows, 2 * block_rows - 1)
        return skewed[:, block_rows - 1 :]

    lag_table = jax.vmap(lag_matrix)(jnp.arange(2 * members))

    def toeplitz_many(offset_grid):
        return lag_table[offset_grid]

    local_times = jnp.stack([position, 2 * members - 1 - position])

    def piece_times(block_count):
        storage = jnp.arange(block_count)
        return jnp.where(storage % 2 == 0, storage // 2, 2 * members - 1 - storage // 2)

    def slab_for(offset_grid, flipped):
        keep = (offset_grid >= 0).astype(jnp.bfloat16)[:, :, None, None]
        mats = toeplitz_many(jnp.maximum(offset_grid, 0)) * keep
        if flipped:
            mats = jnp.swapaxes(mats, 2, 3)
        block_count = offset_grid.shape[1]
        return mats.transpose(0, 2, 1, 3).reshape(2 * block_rows, block_count * block_rows)

    first_f = first_gate.astype(jnp.float32)
    second_f = second_gate.astype(jnp.float32)
    values_f = values_in.astype(jnp.float32)
    cotan_f = cotangent.astype(jnp.float32)
    gated_product = (first_f * second_f).astype(jnp.bfloat16)
    carried = (cotan_f * values_f).astype(jnp.bfloat16)
    piece_rows = lax.all_gather(gated_product, "seq", axis=0, tiled=True)
    block_count = piece_rows.shape[0] // block_rows
    times = piece_times(block_count)
    offset_grid = local_times[:, None] - times[None, :]
    product = jnp.dot(slab_for(offset_grid, False), piece_rows, preferred_element_type=jnp.float32)
    longconv = product.reshape(2, block_rows, channels)
    piece_rows = lax.all_gather(carried, "seq", axis=0, tiled=True)
    block_count = piece_rows.shape[0] // block_rows
    times = piece_times(block_count)
    offset_grid = times[None, :] - local_times[:, None]
    product = jnp.dot(slab_for(offset_grid, True), piece_rows, preferred_element_type=jnp.float32)
    backconv = product.reshape(2, block_rows, channels)
    longconv = longconv.reshape(shard_rows, channels)
    backconv = backconv.reshape(shard_rows, channels)
    skip_scale = skip_gain[None, :]
    mixed_total = longconv + skip_scale * gated_product.astype(jnp.float32)
    output = (values_f * mixed_total).astype(jnp.bfloat16)
    grad_mixed = backconv + skip_scale * carried.astype(jnp.float32)
    grad_first = (grad_mixed * second_f).astype(jnp.bfloat16)
    grad_second = (grad_mixed * first_f).astype(jnp.bfloat16)
    grad_values = (cotan_f * mixed_total).astype(jnp.bfloat16)
    return (output, grad_first, grad_second, grad_values)


def solution(mesh):
    return jax.shard_map(
        on_device,
        mesh=mesh,
        in_specs=(
            P("seq", "ch"),
            P("seq", "ch"),
            P("seq", "ch"),
            P("seq", "ch"),
            P(("ch", "seq")),
            P("ch"),
        ),
        out_specs=(P("seq", "ch"), P("seq", "ch"), P("seq", "ch"), P("seq", "ch")),
        check_vma=False,
    )
```

profile of v0, /device:TPU:64, one launch (start us, length us, event | category | flops | bytes accessed | tf_op | source)
XLA Modules:
  0.0 278.4 jit_solution(13285335274988886201)
XLA Ops:
  7.2 1.7 fusion.14
  9.9 39.3 %all-gather = bf16[32,1,256]{2,1,0:T(2,128)(2,1)S(1)} all-gather(bf16[1,1,256]{2,1,0:T(2,128)(2,1)S(1)} %reshape.244), channel_id=1, replica_groups=mesh['seq'=32,'ch'=16] {'seq'}, dimensions={0}, use_global_device_ids=true | all-gather | bytes 16896 | tf_op jit(solution)/shard_map/all_gather | solution.py:12
  49.3 86.8 %while.1 = (s32[]{:T(128)}, bf16[8320]{0:T(1024)(128)(2,1)S(1)}, s32[64,1]{0,1:T(1,128)S(1)}, bf16[64,256]{1,0:T(8,128)(2,1)S(1)}, s32[]{:T(128)}, /*index=5*/s32[]{:T(128)}) while((s32[]{:T(128)}, bf16[8320]{0:T(1024)(128)(2,1)S(1)}, s32[64,1]{0,1:T(1,128)S(1)}, bf16[64,256]{1,0:T(8,128)(2,1)S(1)}, s32[]{:T(128)}, /*index=5*/s32[]{:T(128)}) %tuple.25), condition=%wide.while_cond, body=%wide.while_body.sunk | while | flops 2 | bytes 3161 | solution.py:16
  49.9 0.7 dynamic-slice.7
  51.3 0.7 dynamic-slice.7
  52.7 0.7 dynamic-slice.7
  54.0 0.7 dynamic-slice.7
  55.4 0.7 dynamic-slice.7
  56.7 0.7 dynamic-slice.7
  58.1 0.7 dynamic-slice.7
  59.4 0.7 dynamic-slice.7
  60.8 0.7 dynamic-slice.7
  62.1 0.7 dynamic-slice.7
  63.5 0.7 dynamic-slice.7
  64.9 0.7 dynamic-slice.7
  66.2 0.7 dynamic-slice.7
  67.6 0.7 dynamic-slice.7
  68.9 0.7 dynamic-slice.7
  70.3 0.7 dynamic-slice.7
  71.6 0.7 dynamic-slice.7
  73.0 0.7 dynamic-slice.7
  74.4 0.7 dynamic-slice.7
  75.7 0.7 dynamic-slice.7
  77.1 0.7 dynamic-slice.7
  78.4 0.7 dynamic-slice.7
  79.8 0.7 dynamic-slice.7
  81.1 0.7 dynamic-slice.7
  82.5 0.7 dynamic-slice.7
  83.8 0.7 dynamic-slice.7
  85.2 0.7 dynamic-slice.7
  86.6 0.7 dynamic-slice.7
  87.9 0.7 dynamic-slice.7
  89.3 0.7 dynamic-slice.7
  90.6 0.7 dynamic-slice.7
  92.0 0.7 dynamic-slice.7
  93.3 0.7 dynamic-slice.7
  94.7 0.7 dynamic-slice.7
  96.1 0.7 dynamic-slice.7
  97.4 0.7 dynamic-slice.7
  98.8 0.7 dynamic-slice.7
  100.1 0.7 dynamic-slice.7
  101.5 0.7 dynamic-slice.7
  102.8 0.7 dynamic-slice.7
  104.2 0.7 dynamic-slice.7
  105.5 0.7 dynamic-slice.7
  106.9 0.7 dynamic-slice.7
  108.3 0.7 dynamic-slice.7
  109.6 0.7 dynamic-slice.7
  111.0 0.7 dynamic-slice.7
  112.3 0.7 dynamic-slice.7
  113.7 0.7 dynamic-slice.7
  120.5 0.7 dynamic-slice.7
  136.6 2.6 copy.15
  139.2 2.2 slice.18
  141.5 15.9 %reshape.209 = bf16[64,128,255]{2,1,0:T(8,128)(2,1)} reshape(bf16[64,32640]{1,0:T(8,128)(2,1)} %slice.18) | data formatting | bytes 8355840 | tf_op jit(solution)/shard_map/vmap()/reshape | solution.py:19
  157.3 3.0 %slice.19 = bf16[64,128,128]{2,1,0:T(8,128)(2,1)S(1)} slice(bf16[64,128,255]{2,1,0:T(8,128)(2,1)} %reshape.209), slice={[0:64], [0:128], [127:255]} | slice | bytes 4194304 | tf_op jit(solution)/shard_map/vmap()/slice | solution.py:20
  160.3 3.0 %gather_fusion = bf16[128,128,128]{2,1,0:T(8,128)(2,1)} fusion(bf16[64,128,128]{2,1,0:T(8,128)(2,1)S(1)} %slice.19, s32[1024]{0:T(1024)S(1)} %pad_clamp_fusion.1), kind=kCustom, calls=%fused_computation | custom fusion | bytes 8389120 | tf_op jit(solution)/shard_map/gather | solution.py:25
  163.5 6.9 %copy_multiply_fusion = bf16[2,64,128,128]{3,1,2,0:T(8,128)(2,1)} fusion(bf16[2,64,128,128]{3,2,1,0:T(8,128)(2,1)} %bitcast.37, bf16[2,64]{1,0:T(2,128)(2,1)S(1)} %get-tuple-element.26), kind=kLoop, calls=%fused_computation.9 | loop fusion | flops 2097152 | bytes 8388864 | tf_op jit(solution)/shard_map/mul | solution.py:35
  170.4 6.8 %fusion.17 = (bf16[256,256]{1,0:T(8,128)(2,1)}, bf16[256,256]{1,0:T(8,128)(2,1)}, bf16[256,256]{1,0:T(8,128)(2,1)}) fusion(bf16[256,256]{1,0:T(8,128)(2,1)S(1)} %copy-done.4, bf16[256,256]{1,0:T(8,128)(2,1)S(1)} %copy-done.5, bf16[256,256]{1,0:T(8,128)(2,1)S(1)} %copy-done, f32[256]{0:T(256)S(1)} %copy-done.6, ...), kind=kOutput, calls=%fused_computation.24 | convolution fusion | flops 1074462720 | bytes 9176064 | tf_op jit(solution)/shard_map/dot_general | solution.py:51
  177.2 3.0 %gather_fusion.1 = bf16[128,128,128]{2,1,0:T(8,128)(2,1)} fusion(bf16[64,128,128]{2,1,0:T(8,128)(2,1)S(1)} %slice.19, s32[1024]{0:T(1024)S(1)} %pad_clamp_fusion), kind=kCustom, calls=%fused_computation.1 | custom fusion | bytes 8389120 | tf_op jit(solution)/shard_map/gather | solution.py:25
  180.3 6.6 %copy.13 = bf16[2,64,128,128]{2,1,3,0:T(8,128)(2,1)} copy(bf16[2,64,128,128]{3,2,1,0:T(8,128)(2,1)} %bitcast.38) | data formatting | bytes 8388608 | tf_op jit(solution)/shard_map/gather | solution.py:25
  186.9 4.5 %broadcast_multiply_fusion = bf16[2,64,128,128]{2,1,3,0:T(8,128)(2,1)} fusion(bf16[2,64,128,128]{2,1,3,0:T(8,128)(2,1)} %copy.13, bf16[2,64]{1,0:T(2,128)(2,1)S(1)} %get-tuple-element.25), kind=kLoop, calls=%fused_computation.10 | loop fusion | flops 2097152 | bytes 8388864 | tf_op jit(solution)/shard_map/mul | solution.py:35
  191.4 73.5 %all-gather.6.cloned.1.call-done = bf16[8192,256]{1,0:T(8,128)(2,1)} async-done(((bf16[256,256]{1,0:T(8,128)(2,1)}), bf16[8192,256]{1,0:T(8,128)(2,1)}) %all-gather.6.cloned.1.call-update) | async-done | bytes 4194320 | tf_op jit(solution)/shard_map/all_gather | solution.py:53
  264.9 6.7 %fusion.13 = (bf16[256,256]{1,0:T(8,128)(2,1)}, bf16[256,256]{1,0:T(8,128)(2,1)}) fusion(bf16[256,256]{1,0:T(8,128)(2,1)S(1)} %copy-done.2, bf16[256,256]{1,0:T(8,128)(2,1)S(1)} %copy-done.1, bf16[256,256]{1,0:T(8,128)(2,1)S(1)} %copy-done.3, f32[256]{0:T(256)S(1)} %copy-done.6, bf16[8192,256]{1,0:T(8,128)(2,1)} %all-gather.6.cloned.1.call-done, ...), kind=kOutput, calls=%fused_computation.20 | convolution fusion | flops 1074331648 | bytes 9044992 | tf_op jit(solution)/shard_map/dot_general | solution.py:57
  (242 shorter events, 52.4 us)
Async XLA Ops:
  7.2 163.2 %all-gather.4.cloned.1.call-start = ((), (), s32[]{:S(2)}) async-start(), calls=%async_computation | async-start | bytes 4325376 | tf_op jit(solution)/shard_map/all_gather | solution.py:47
  8.9 256.0 %all-gather.6.cloned.1.call-start = ((), (), s32[]{:S(2)}) async-start(), calls=%async_computation.1 | async-start | bytes 4325376 | tf_op jit(solution)/shard_map/all_gather | solution.py:53
  163.4 6.9 %copy-start = (bf16[256,256]{1,0:T(8,128)(2,1)S(1)}, bf16[256,256]{1,0:T(8,128)(2,1)}, u32[]{:S(2)}) copy-start(bf16[256,256]{1,0:T(8,128)(2,1)} %fusion.14) | copy-start | bytes 393220
  163.4 6.9 %copy-start.4 = (bf16[256,256]{1,0:T(8,128)(2,1)S(1)}, bf16[256,256]{1,0:T(8,128)(2,1)}, u32[]{:S(2)}) copy-start(bf16[256,256]{1,0:T(8,128)(2,1)} %param.9) | copy-start | bytes 393220
  163.4 6.9 %copy-start.5 = (bf16[256,256]{1,0:T(8,128)(2,1)S(1)}, bf16[256,256]{1,0:T(8,128)(2,1)}, u32[]{:S(2)}) copy-start(bf16[256,256]{1,0:T(8,128)(2,1)} %param.8) | copy-start | bytes 393220
  163.4 6.9 %copy-start.6 = (f32[256]{0:T(256)S(1)}, f32[256]{0:T(256)}, u32[]{:S(2)}) copy-start(f32[256]{0:T(256)} %param.11) | copy-start | bytes 3076
  186.9 78.0 %copy-start.1 = (bf16[256,256]{1,0:T(8,128)(2,1)S(1)}, bf16[256,256]{1,0:T(8,128)(2,1)}, u32[]{:S(2)}) copy-start(bf16[256,256]{1,0:T(8,128)(2,1)} %param.7) | copy-start | bytes 393220
  186.9 78.0 %copy-start.2 = (bf16[256,256]{1,0:T(8,128)(2,1)S(1)}, bf16[256,256]{1,0:T(8,128)(2,1)}, u32[]{:S(2)}) copy-start(bf16[256,256]{1,0:T(8,128)(2,1)} %param.6) | copy-start | bytes 393220
  186.9 78.0 %copy-start.3 = (bf16[256,256]{1,0:T(8,128)(2,1)S(1)}, bf16[256,256]{1,0:T(8,128)(2,1)}, u32[]{:S(2)}) copy-start(bf16[256,256]{1,0:T(8,128)(2,1)} %get-tuple-element.22) | copy-start | bytes 393220
Sparse Core Ops, SparseCore 0:
  11.7 90.9 all-gather.3
  177.3 87.5 all-gather.5
where the time goes:
time: 280 us; the launch traced here: 278 us
  local copies, waits for them, and re-layouts  124 us (44%)
  waiting for transfers between devices  73.5 us (26%)
  blocking collectives  39.3 us (14%)
  between operations  14.1 us (5%)
  matrix products  13.5 us (5%)
  other arithmetic  13.4 us (5%)
    gather x256, local copies, waits for them, and re-layouts  86.3 us
    all_gather x1, waiting for transfers between devices, on_device(): piece_rows = lax.all_gather(carried, 'seq', axis=0, tiled=True)  73.5 us
    all_gather x1, blocking collectives, on_device(): filter_taps = lax.all_gather(filters, 'seq', axis=0, tiled=True)  39.3 us
    reshape x1, local copies, waits for them, and re-layouts, lag_matrix(): tiled[:block_rows * (2 * block_rows - 1)]  15.9 us
    gather x3, local copies, waits for them, and re-layouts, toeplitz_many(): return lag_table[offset_grid]  12.7 us
    mul x2, other arithmetic, slab_for(): mats = toeplitz_many(jnp.maximum(offset_grid, 0)) * keep  11.4 us
    dot_general x1, matrix products, on_device(): jnp.dot(slab_for(offset_grid, False), piece_rows, preferred_element_type=...  6.77 us
    dot_general x1, matrix products, on_device(): jnp.dot(slab_for(offset_grid, True), piece_rows, preferred_element_type=j...  6.72 us
  transfers between devices with their start and end apart: 2, of which 1 were waited for; matrix products, arithmetic and copies ran while one was open for 49% of the time, Pallas kernels for 0%

commit v1 on v0

v1 whole, which is shorter than its diff:
```python
import functools

import jax
import jax.numpy as jnp
from jax import lax
from jax.experimental import pallas as pl
from jax.experimental.pallas import tpu as pltpu
from jax.sharding import PartitionSpec as P

BF16 = jnp.bfloat16
F32 = jnp.float32
SUB = 8
ROWS = 2 * SUB
NT = (((1,), (1,)), ((), ()))


def select_matrix(size, flipped):
    row = lax.broadcasted_iota(jnp.int32, (size, size), 0)
    col = lax.broadcasted_iota(jnp.int32, (size, size), 1)
    hit = (row + col == size - 1) if flipped else (row == col)
    return jnp.where(hit, 1.0, 0.0).astype(BF16)


def kernel(
    n,
    fg_hbm, sg_hbm, vi_hbm, ct_hbm, taps_ref, skip_ref,
    fwd_ref, bwd_ref,
    fields, tap_buf, send1, recv1, xbuf, slab, acc, send2, recv2,
    in_sem, tap_send, tap_recv, send1_sem, recv1_sem, send2_sem, recv2_sem,
):
    me = lax.axis_index("seq")
    half = fg_hbm.shape[0] // 2
    chunk = 2 * half
    channels = fg_hbm.shape[1]

    def each_peer(visit):
        def body(k, carry):
            visit(lax.rem(me + k, n))
            return carry
        lax.fori_loop(1, n, body, 0)

    loads = [
        pltpu.make_async_copy(src, fields.at[k], in_sem.at[k])
        for k, src in enumerate((fg_hbm, sg_hbm, ct_hbm, vi_hbm))
    ]
    for load in loads:
        load.start()
    barrier = pltpu.get_barrier_semaphore()
    each_peer(lambda peer: pl.semaphore_signal(barrier, inc=1, device_id={"seq": peer}))

    tap_buf[0] = jnp.zeros((1, chunk), F32)
    tap_buf[me + 1] = taps_ref[...]

    plain = select_matrix(chunk, False)
    flipped = select_matrix(chunk, True)
    loads[0].wait()
    loads[1].wait()
    gated = (fields[0].astype(F32) * fields[1].astype(F32)).astype(BF16)
    across = plain if channels == chunk else select_matrix(channels, False)
    gated_t = lax.dot_general(across, gated, NT, preferred_element_type=F32)
    loads[2].wait()
    loads[3].wait()
    carried = (fields[2].astype(F32) * fields[3].astype(F32)).astype(BF16)
    carried_r = jnp.dot(flipped, carried, preferred_element_type=F32).astype(BF16)
    carried_t = lax.dot_general(across, carried_r, NT, preferred_element_type=F32)
    both = jnp.concatenate(
        [gated_t.reshape(n, SUB, chunk), carried_t.reshape(n, SUB, chunk)], axis=1
    )
    send1[...] = both.astype(BF16)
    recv1[me] = send1[me]

    pl.semaphore_wait(barrier, n - 1)

    def send_taps(peer):
        pltpu.make_async_remote_copy(
            src_ref=taps_ref, dst_ref=tap_buf.at[me + 1],
            send_sem=tap_send, recv_sem=tap_recv, device_id={"seq": peer},
        ).start()

    def send_first(peer):
        pltpu.make_async_remote_copy(
            src_ref=send1.at[peer], dst_ref=recv1.at[me],
            send_sem=send1_sem, recv_sem=recv1_sem, device_id={"seq": peer},
        ).start()

    def send_second(peer):
        pltpu.make_async_remote_copy(
            src_ref=send2.at[peer], dst_ref=recv2.at[me],
            send_sem=send2_sem, recv_sem=recv2_sem, device_id={"seq": peer},
        ).start()

    def whole(buf, send_sem, recv_sem):
        part = buf.at[pl.ds(0, n - 1)]
        return pltpu.make_async_remote_copy(
            src_ref=part, dst_ref=part, send_sem=send_sem, recv_sem=recv_sem,
            device_id={"seq": lax.rem(me + 1, n)},
        )

    each_peer(send_taps)
    each_peer(send_first)

    all_taps = whole(tap_buf, tap_send, tap_recv)
    all_taps.wait_recv()
    slab[:, 0:half] = jnp.zeros((half, half), BF16)

    def build(j, carry):
        window = jnp.concatenate([tap_buf[j][:, half:], tap_buf[j + 1]], axis=1)
        window = jnp.broadcast_to(window, (ROWS, half + chunk))
        skewed = pltpu.roll(window, 0, 1, stride=1, stride_axis=0)
        for k in range(half // ROWS):
            moved = skewed if k == 0 else pltpu.roll(skewed, k * ROWS, 1)
            slab[k * ROWS:(k + 1) * ROWS, pl.ds(pl.multiple_of(j * chunk + half, half), chunk)] = (
                moved[:, half:].astype(BF16)
            )
        return carry

    lax.fori_loop(0, n, build, 0)

    lane = lax.broadcasted_iota(jnp.int32, (ROWS, channels), 1)
    row = lax.broadcasted_iota(jnp.int32, (ROWS, channels), 0)
    mine = lane == me * SUB + lax.rem(row, SUB)
    gains = jnp.sum(jnp.where(mine, skip_ref[...], 0.0), axis=1, keepdims=True)

    first = whole(recv1, send1_sem, recv1_sem)
    first.wait_recv()
    for block in range(2 * n):
        source, side = (block, 0) if block < n else (2 * n - 1 - block, 1)
        piece = recv1[source, :, side * half:(side + 1) * half]
        pair, place = block // 2, block % 2
        at = (slice(pair * ROWS, (pair + 1) * ROWS), slice(place * half, (place + 1) * half))
        xbuf[at] = piece
        acc[at] = gains * piece.astype(F32)

    total = n * ROWS
    groups = 4
    per = n // groups
    for g in range(groups):
        depth = total - g * per * ROWS

        def step(d, carry):
            top = slab[:, pl.ds(pl.multiple_of(d * chunk + half, half), chunk)]
            low = slab[:, pl.ds(pl.multiple_of(d * chunk, chunk), chunk)]
            lags = jnp.concatenate([top, low], axis=0)
            term = jnp.dot(xbuf[0:depth, :], lags, preferred_element_type=F32)
            rows = pl.ds(pl.multiple_of(d * ROWS, ROWS), depth)
            acc[rows, :] = acc[rows, :] + term
            return carry

        lax.fori_loop(g * per, (g + 1) * per, step, 0)

    for dst in range(n):
        left, right = dst, 2 * n - 1 - dst
        pieces = [
            acc[(b // 2) * ROWS:(b // 2 + 1) * ROWS, (b % 2) * half:(b % 2 + 1) * half]
            for b in (left, right)
        ]
        send2[dst] = jnp.concatenate(pieces, axis=1).astype(BF16)
    recv2[me] = send2[me]
    each_peer(send_second)
    second = whole(recv2, send2_sem, recv2_sem)
    second.wait_recv()
    back = recv2[...].astype(F32)
    fwd_t = back[:, 0:SUB, :].reshape(channels, chunk).astype(BF16)
    bwd_t = back[:, SUB:, :].reshape(channels, chunk).astype(BF16)
    fwd_ref[...] = lax.dot_general(plain, fwd_t, NT, preferred_element_type=F32).astype(BF16)
    bwd_ref[...] = lax.dot_general(flipped, bwd_t, NT, preferred_element_type=F32).astype(BF16)
    all_taps.wait_send()
    first.wait_send()
    second.wait_send()


def on_device(n, first_gate, second_gate, values_in, cotangent, filters, skip_gain):
    chunk, channels = first_gate.shape
    half = chunk // 2
    taps = filters.astype(F32).reshape(1, chunk)
    anywhere = pl.BlockSpec(memory_space=pl.ANY)
    in_vmem = pl.BlockSpec(memory_space=pltpu.VMEM)
    result = jax.ShapeDtypeStruct((chunk, channels), BF16)
    message = pltpu.VMEM((n, ROWS, chunk), BF16)
    mixed_total, grad_mixed = pl.pallas_call(
        functools.partial(kernel, n),
        out_shape=(result, result),
        in_specs=[anywhere] * 4 + [in_vmem] * 2,
        out_specs=(in_vmem, in_vmem),
        scratch_shapes=[
            pltpu.VMEM((4, chunk, channels), BF16),
            pltpu.VMEM((n + 1, 1, chunk), F32),
            message,
            message,
            pltpu.VMEM((n * ROWS, chunk), BF16),
            pltpu.VMEM((half, half + n * chunk), BF16),
            pltpu.VMEM((n * ROWS + n * ROWS // 4, chunk), F32),
            message,
            message,
            pltpu.SemaphoreType.DMA((4,)),
            pltpu.SemaphoreType.DMA,
            pltpu.SemaphoreType.DMA,
            pltpu.SemaphoreType.DMA,
            pltpu.SemaphoreType.DMA,
            pltpu.SemaphoreType.DMA,
            pltpu.SemaphoreType.DMA,
        ],
        compiler_params=pltpu.CompilerParams(
            collective_id=0, has_side_effects=True, vmem_limit_bytes=32 * 1024 * 1024
        ),
    )(first_gate, second_gate, values_in, cotangent, taps, skip_gain.reshape(1, channels))
    mixed_total = mixed_total.astype(F32)
    grad_mixed = grad_mixed.astype(F32)
    output = (values_in.astype(F32) * mixed_total).astype(BF16)
    grad_first = (grad_mixed * second_gate.astype(F32)).astype(BF16)
    grad_second = (grad_mixed * first_gate.astype(F32)).astype(BF16)
    grad_values = (cotangent.astype(F32) * mixed_total).astype(BF16)
    return (output, grad_first, grad_second, grad_values)


def solution(mesh):
    rows = P("seq", "ch")
    return jax.shard_map(
        functools.partial(on_device, mesh.shape["seq"]),
        mesh=mesh,
        in_specs=(rows, rows, rows, rows, P(("ch", "seq")), P("ch")),
        out_specs=(rows, rows, rows, rows),
        check_vma=False,
    )
```

time: 280 us -> 42.3 us (0.15)
  the two profiles are of different devices: /device:TPU:64 before, /device:TPU:256 now
where the time goes in v1:
time: 42.3 us; the launch traced here: 42.1 us
  Pallas kernels  35.6 us (84%)
  local copies, waits for them, and re-layouts  4.94 us (12%)
  other arithmetic  0.89 us (2%)
  between operations  0.65 us (2%)
    pallas_call x1, Pallas kernels, on_device(): pl.pallas_call(functools.partial(kernel, n), out_shape=(result, result),...  35.6 us
    unnamed x12, local copies, waits for them, and re-layouts  4.94 us
    convert_element_type x1, other arithmetic, on_device(): grad_values = (cotangent.astype(F32) * mixed_total).astype(BF16)  0.89 us

profile of v1, /device:TPU:256, one launch (start us, length us, event | category | flops | bytes accessed | tf_op | source)
XLA Modules:
  0.0 42.1 jit_solution(14637160521779099239)
XLA Ops:
  0.6 0.0 copy-start.5
  0.6 0.6 %copy-done.5 = bf16[256]{0:T(256)(128)(2,1)S(1)} copy-done((bf16[256]{0:T(256)(128)(2,1)S(1)}, bf16[256]{0:T(256)(128)(2,1)}, u32[]{:S(2)}) %copy-start.5) | copy-done | bytes 536
  1.3 0.0 copy-start.4
  1.3 0.7 %copy-done.4 = f32[256]{0:T(256)S(1)} copy-done((f32[256]{0:T(256)S(1)}, f32[256]{0:T(256)}, u32[]{:S(2)}) %copy-start.4) | copy-done | bytes 1048
  2.0 0.0 copy-start
  2.0 0.9 %copy-done = bf16[256,256]{1,0:T(8,128)(2,1)S(1)} copy-done((bf16[256,256]{1,0:T(8,128)(2,1)S(1)}, bf16[256,256]{1,0:T(8,128)(2,1)}, u32[]{:S(2)}) %copy-start) | copy-done | bytes 131096
  2.9 0.0 copy-start.1
  2.9 0.9 %copy-done.1 = bf16[256,256]{1,0:T(8,128)(2,1)S(1)} copy-done((bf16[256,256]{1,0:T(8,128)(2,1)S(1)}, bf16[256,256]{1,0:T(8,128)(2,1)}, u32[]{:S(2)}) %copy-start.1) | copy-done | bytes 131096
  3.8 0.0 copy-start.2
  3.8 0.9 %copy-done.2 = bf16[256,256]{1,0:T(8,128)(2,1)S(1)} copy-done((bf16[256,256]{1,0:T(8,128)(2,1)S(1)}, bf16[256,256]{1,0:T(8,128)(2,1)}, u32[]{:S(2)}) %copy-start.2) | copy-done | bytes 131096
  4.7 0.0 copy-start.3
  4.7 0.9 %copy-done.3 = bf16[256,256]{1,0:T(8,128)(2,1)S(1)} copy-done((bf16[256,256]{1,0:T(8,128)(2,1)S(1)}, bf16[256,256]{1,0:T(8,128)(2,1)}, u32[]{:S(2)}) %copy-start.3) | copy-done | bytes 131096
  5.6 35.6 %shard_map.93 = (bf16[256,256]{1,0:T(8,128)(2,1)S(1)}, bf16[256,256]{1,0:T(8,128)(2,1)S(1)}) custom-call(bf16[256,256]{1,0:T(8,128)(2,1)S(1)} %copy-done, bf16[256,256]{1,0:T(8,128)(2,1)S(1)} %copy-done.1, bf16[256,256]{1,0:T(8,128)(2,1)S(1)} %copy-done.2, bf16[256,256]{1,0:T(8,128)(2,1)S(1)} %copy-done.3, f32[1,256]{1,0:T(1,128)S(1)} %bitcast.3, ...), custom_call_target="tpu_custom_call" | custom-call | tf_op jit(solution)/shard_map/pallas_call | solution.py:180
  41.2 0.9 %fusion.1 = (bf16[256,256]{1,0:T(8,128)(2,1)}, bf16[256,256]{1,0:T(8,128)(2,1)}, bf16[256,256]{1,0:T(8,128)(2,1)}, bf16[256,256]{1,0:T(8,128)(2,1)}) fusion(bf16[256,256]{1,0:T(8,128)(2,1)S(1)} %get-tuple-element.6, bf16[256,256]{1,0:T(8,128)(2,1)S(1)} %copy-done.3, bf16[256,256]{1,0:T(8,128)(2,1)S(1)} %copy-done.2, bf16[256,256]{1,0:T(8,128)(2,1)S(1)} %copy-done.1, ...), kind=kLoop, calls=%fused_computation.5 | loop fusion | flops 917504 | bytes 1310720 | tf_op jit(solution)/shard_map/convert_element_type | solution.py:212
  (1 shorter events, 0.0 us)
Async XLA Ops:
  0.6 0.7 %copy-start.5 = (bf16[256]{0:T(256)(128)(2,1)S(1)}, bf16[256]{0:T(256)(128)(2,1)}, u32[]{:S(2)}) copy-start(bf16[256]{0:T(256)(128)(2,1)} %param.10) | copy-start | bytes 1540
  1.3 0.7 %copy-start.4 = (f32[256]{0:T(256)S(1)}, f32[256]{0:T(256)}, u32[]{:S(2)}) copy-start(f32[256]{0:T(256)} %param.11) | copy-start | bytes 3076
  2.0 0.9 %copy-start = (bf16[256,256]{1,0:T(8,128)(2,1)S(1)}, bf16[256,256]{1,0:T(8,128)(2,1)}, u32[]{:S(2)}) copy-start(bf16[256,256]{1,0:T(8,128)(2,1)} %fg_hbm.1) | copy-start | bytes 393220
  2.9 0.9 %copy-start.1 = (bf16[256,256]{1,0:T(8,128)(2,1)S(1)}, bf16[256,256]{1,0:T(8,128)(2,1)}, u32[]{:S(2)}) copy-start(bf16[256,256]{1,0:T(8,128)(2,1)} %sg_hbm.1) | copy-start | bytes 393220
  3.8 0.9 %copy-start.2 = (bf16[256,256]{1,0:T(8,128)(2,1)S(1)}, bf16[256,256]{1,0:T(8,128)(2,1)}, u32[]{:S(2)}) copy-start(bf16[256,256]{1,0:T(8,128)(2,1)} %vi_hbm.1) | copy-start | bytes 393220
  4.7 0.9 %copy-start.3 = (bf16[256,256]{1,0:T(8,128)(2,1)S(1)}, bf16[256,256]{1,0:T(8,128)(2,1)}, u32[]{:S(2)}) copy-start(bf16[256,256]{1,0:T(8,128)(2,1)} %ct_hbm.1) | copy-start | bytes 393220

commit v2 on v1

--- a/solution.py
+++ b/solution.py
@@ -23,9 +23,9 @@
 
 def kernel(
     n,
-    fg_hbm, sg_hbm, vi_hbm, ct_hbm, taps_ref, skip_ref,
-    fwd_ref, bwd_ref,
-    fields, tap_buf, send1, recv1, xbuf, slab, acc, send2, recv2,
+    fg_hbm, sg_hbm, vi_hbm, ct_hbm, taps_hbm, skip_hbm,
+    fwd_ref, bwd_ref, fg, sg, vi, ct,
+    tap_own, skip_own, tap_buf, send1, recv1, xbuf, slab, acc, send2, recv2,
     in_sem, tap_send, tap_recv, send1_sem, recv1_sem, send2_sem, recv2_sem,
 ):
     me = lax.axis_index("seq")
@@ -39,28 +39,32 @@
             return carry
         lax.fori_loop(1, n, body, 0)
 
+    barrier = pltpu.get_barrier_semaphore()
+    each_peer(lambda peer: pl.semaphore_signal(barrier, inc=1, device_id={"seq": peer}))
     loads = [
-        pltpu.make_async_copy(src, fields.at[k], in_sem.at[k])
-        for k, src in enumerate((fg_hbm, sg_hbm, ct_hbm, vi_hbm))
+        pltpu.make_async_copy(src, dst, in_sem.at[k])
+        for k, (src, dst) in enumerate(
+            ((taps_hbm, tap_own), (fg_hbm, fg), (sg_hbm, sg), (ct_hbm, ct), (vi_hbm, vi), (skip_hbm, skip_own))
+        )
     ]
     for load in loads:
         load.start()
-    barrier = pltpu.get_barrier_semaphore()
-    each_peer(lambda peer: pl.semaphore_signal(barrier, inc=1, device_id={"seq": peer}))
 
     tap_buf[0] = jnp.zeros((1, chunk), F32)
-    tap_buf[me + 1] = taps_ref[...]
+    loads[0].wait()
+    own = tap_own[...].astype(F32)
+    tap_buf[me + 1] = jnp.concatenate([own[0:1], own[1:2]], axis=1)
 
     plain = select_matrix(chunk, False)
     flipped = select_matrix(chunk, True)
-    loads[0].wait()
     loads[1].wait()
-    gated = (fields[0].astype(F32) * fields[1].astype(F32)).astype(BF16)
+    loads[2].wait()
+    gated = (fg[...].astype(F32) * sg[...].astype(F32)).astype(BF16)
     across = plain if channels == chunk else select_matrix(channels, False)
     gated_t = lax.dot_general(across, gated, NT, preferred_element_type=F32)
-    loads[2].wait()
     loads[3].wait()
-    carried = (fields[2].astype(F32) * fields[3].astype(F32)).astype(BF16)
+    loads[4].wait()
+    carried = (ct[...].astype(F32) * vi[...].astype(F32)).astype(BF16)
     carried_r = jnp.dot(flipped, carried, preferred_element_type=F32).astype(BF16)
     carried_t = lax.dot_general(across, carried_r, NT, preferred_element_type=F32)
     both = jnp.concatenate(
@@ -73,7 +77,7 @@
 
     def send_taps(peer):
         pltpu.make_async_remote_copy(
-            src_ref=taps_ref, dst_ref=tap_buf.at[me + 1],
+            src_ref=tap_buf.at[me + 1], dst_ref=tap_buf.at[me + 1],
             send_sem=tap_send, recv_sem=tap_recv, device_id={"seq": peer},
         ).start()
 
@@ -105,21 +109,18 @@
 
     def build(j, carry):
         window = jnp.concatenate([tap_buf[j][:, half:], tap_buf[j + 1]], axis=1)
-        window = jnp.broadcast_to(window, (ROWS, half + chunk))
+        window = jnp.broadcast_to(window, (half, half + chunk))
         skewed = pltpu.roll(window, 0, 1, stride=1, stride_axis=0)
-        for k in range(half // ROWS):
-            moved = skewed if k == 0 else pltpu.roll(skewed, k * ROWS, 1)
-            slab[k * ROWS:(k + 1) * ROWS, pl.ds(pl.multiple_of(j * chunk + half, half), chunk)] = (
-                moved[:, half:].astype(BF16)
-            )
+        slab[:, pl.ds(pl.multiple_of(j * chunk + half, half), chunk)] = skewed[:, half:].astype(BF16)
         return carry
 
-    lax.fori_loop(0, n, build, 0)
+    lax.fori_loop(0, n, build, 0, unroll=4)
 
     lane = lax.broadcasted_iota(jnp.int32, (ROWS, channels), 1)
     row = lax.broadcasted_iota(jnp.int32, (ROWS, channels), 0)
     mine = lane == me * SUB + lax.rem(row, SUB)
-    gains = jnp.sum(jnp.where(mine, skip_ref[...], 0.0), axis=1, keepdims=True)
+    loads[5].wait()
+    gains = jnp.sum(jnp.where(mine, skip_own[...], 0.0), axis=1, keepdims=True)
 
     first = whole(recv1, send1_sem, recv1_sem)
     first.wait_recv()
@@ -132,21 +133,12 @@
         acc[at] = gains * piece.astype(F32)
 
     total = n * ROWS
-    groups = 4
-    per = n // groups
-    for g in range(groups):
-        depth = total - g * per * ROWS
-
-        def step(d, carry):
-            top = slab[:, pl.ds(pl.multiple_of(d * chunk + half, half), chunk)]
-            low = slab[:, pl.ds(pl.multiple_of(d * chunk, chunk), chunk)]
-            lags = jnp.concatenate([top, low], axis=0)
-            term = jnp.dot(xbuf[0:depth, :], lags, preferred_element_type=F32)
-            rows = pl.ds(pl.multiple_of(d * ROWS, ROWS), depth)
-            acc[rows, :] = acc[rows, :] + term
-            return carry
-
-        lax.fori_loop(g * per, (g + 1) * per, step, 0)
+    for d in range(n):
+        top = slab[:, d * chunk + half:(d + 1) * chunk + half]
+        low = slab[:, d * chunk:(d + 1) * chunk]
+        lags = jnp.concatenate([top, low], axis=0)
+        term = jnp.dot(xbuf[0:total - d * ROWS, :], lags, preferred_element_type=F32)
+        acc[d * ROWS:total, :] = acc[d * ROWS:total, :] + term
 
     for dst in range(n):
         left, right = dst, 2 * n - 1 - dst
@@ -172,27 +164,28 @@
 def on_device(n, first_gate, second_gate, values_in, cotangent, filters, skip_gain):
     chunk, channels = first_gate.shape
     half = chunk // 2
-    taps = filters.astype(F32).reshape(1, chunk)
-    anywhere = pl.BlockSpec(memory_space=pl.ANY)
+    taps = filters.reshape(2, half)
+    in_hbm = pl.BlockSpec(memory_space=pltpu.HBM)
     in_vmem = pl.BlockSpec(memory_space=pltpu.VMEM)
-    result = jax.ShapeDtypeStruct((chunk, channels), BF16)
+    result = pltpu.VMEM((chunk, channels), BF16)
     message = pltpu.VMEM((n, ROWS, chunk), BF16)
-    mixed_total, grad_mixed = pl.pallas_call(
+    mixed_total, grad_mixed, first_gate, second_gate, values_in, cotangent = pl.pallas_call(
         functools.partial(kernel, n),
-        out_shape=(result, result),
-        in_specs=[anywhere] * 4 + [in_vmem] * 2,
-        out_specs=(in_vmem, in_vmem),
+        out_shape=(result,) * 6,
+        in_specs=[in_hbm] * 6,
+        out_specs=(in_vmem,) * 6,
         scratch_shapes=[
-            pltpu.VMEM((4, chunk, channels), BF16),
+            pltpu.VMEM((2, half), BF16),
+            pltpu.VMEM((1, channels), F32),
             pltpu.VMEM((n + 1, 1, chunk), F32),
             message,
             message,
             pltpu.VMEM((n * ROWS, chunk), BF16),
             pltpu.VMEM((half, half + n * chunk), BF16),
-            pltpu.VMEM((n * ROWS + n * ROWS // 4, chunk), F32),
-            message,
-            message,
-            pltpu.SemaphoreType.DMA((4,)),
+            pltpu.VMEM((n * ROWS, chunk), F32),
+            message,
+            message,
+            pltpu.SemaphoreType.DMA((6,)),
             pltpu.SemaphoreType.DMA,
             pltpu.SemaphoreType.DMA,
             pltpu.SemaphoreType.DMA,
@@ -203,7 +196,10 @@
         compiler_params=pltpu.CompilerParams(
             collective_id=0, has_side_effects=True, vmem_limit_bytes=32 * 1024 * 1024
         ),
-    )(first_gate, second_gate, values_in, cotangent, taps, skip_gain.reshape(1, channels))
+    )(*[
+        pltpu.with_memory_space_constraint(x, pltpu.HBM)
+        for x in (first_gate, second_gate, values_in, cotangent, taps, skip_gain.reshape(1, channels))
+    ])
     mixed_total = mixed_total.astype(F32)
     grad_mixed = grad_mixed.astype(F32)
     output = (values_in.astype(F32) * mixed_total).astype(BF16)

time: 42.3 us -> 30.2 us (0.71)
  the two profiles are of different devices: /device:TPU:256 before, /device:TPU:2 now
where the time goes in v2:
time: 30.2 us; the launch traced here: 30.1 us
  Pallas kernels  28.6 us (95%)
  other arithmetic  0.88 us (3%)
  between operations  0.64 us (2%)
    pallas_call x1, Pallas kernels, on_device(): pl.pallas_call(functools.partial(kernel, n), out_shape=(result,) * 6, in_...  28.6 us
    convert_element_type x1, other arithmetic, on_device(): grad_values = (cotangent.astype(F32) * mixed_total).astype(BF16)  0.88 us

profile of v2, /device:TPU:2, one launch (start us, length us, event | category | flops | bytes accessed | tf_op | source)
XLA Modules:
  0.0 30.1 jit_solution(13399493916800492252)
XLA Ops:
  0.6 28.6 %shard_map.93 = (bf16[256,256]{1,0:T(8,128)(2,1)S(1)}, bf16[256,256]{1,0:T(8,128)(2,1)S(1)}, bf16[256,256]{1,0:T(8,128)(2,1)S(1)}, bf16[256,256]{1,0:T(8,128)(2,...) custom-call(bf16[256,256]{1,0:T(8,128)(2,1)} %fg_hbm.1, bf16[256,256]{1,0:T(8,128)(2,1)} %sg_hbm.1, ...), custom_call_target="tpu_custom_call" | custom-call | tf_op jit(solution)/shard_map/pallas_call | solution.py:172
  29.2 0.9 %fusion.1 = (bf16[256,256]{1,0:T(8,128)(2,1)}, bf16[256,256]{1,0:T(8,128)(2,1)}, bf16[256,256]{1,0:T(8,128)(2,1)}, bf16[256,256]{1,0:T(8,128)(2,1)}) fusion(bf16[256,256]{1,0:T(8,128)(2,1)S(1)} %get-tuple-element.11, bf16[256,256]{1,0:T(8,128)(2,1)S(1)} %get-tuple-element.15, bf16[256,256]{1,0:T(8,128)(2,1)S(1)} %get-tuple-element.10, ...), kind=kLoop, calls=%fused_computation.5 | loop fusion | flops 917504 | bytes 1310720 | tf_op jit(solution)/shard_map/convert_element_type | solution.py:208

commit v3 on v2

v3 whole, which is shorter than its diff:
```python
import functools

import jax
import jax.numpy as jnp
from jax import lax
from jax.experimental import pallas as pl
from jax.experimental.pallas import tpu as pltpu
from jax.sharding import PartitionSpec as P

BF16 = jnp.bfloat16
F32 = jnp.float32
SUB = 8
LINES = 4
NT = (((1,), (1,)), ((), ()))


def select_matrix(size, flipped):
    row = lax.broadcasted_iota(jnp.int32, (size, size), 0)
    col = lax.broadcasted_iota(jnp.int32, (size, size), 1)
    hit = (row + col == size - 1) if flipped else (row == col)
    return jnp.where(hit, 1.0, 0.0).astype(BF16)


def ring(step, size):
    return min(step, size - step)


def far_first(n):
    size = n // LINES
    steps = [(dx, dy) for dx in range(LINES) for dy in range(size)][1:]
    return sorted(steps, key=lambda s: (-ring(s[1], size), -ring(s[0], LINES), s))


def corner_first(n):
    size = n // LINES
    return sorted(range(n), key=lambda d: (ring(d % size, size) * 2 + ring(d // size, LINES) * 2 + (d % size > size // 2), d))


def kernel(
    n,
    fg_hbm, sg_hbm, vi_hbm, ct_hbm, taps_hbm, skip_hbm,
    fwd_ref, bwd_ref, fg, sg, vi, ct,
    tap_own, skip_own, tap_buf, send1, recv1, xbuf, slab, acc, send2, recv2,
    in_sem, tap_send, tap_recv, send1_sem, recv1_sem, send2_sem, recv2_sem,
):
    me = lax.axis_index("seq")
    half = fg_hbm.shape[0] // 2
    chunk = 2 * half
    channels = fg_hbm.shape[1]
    size = n // LINES
    line, place = me // size, lax.rem(me, size)

    def each_far_first(visit):
        for dx, dy in far_first(n):
            visit(lax.rem(line + dx, LINES) * size + lax.rem(place + dy, size))

    def each_corner_first(visit):
        for peer in corner_first(n):
            @pl.when(me != peer)
            def _(peer=peer):
                visit(peer)

    barrier = pltpu.get_barrier_semaphore()
    each_far_first(lambda peer: pl.semaphore_signal(barrier, inc=1, device_id={"seq": peer}))
    loads = [
        pltpu.make_async_copy(src, dst, in_sem.at[k])
        for k, (src, dst) in enumerate(
            ((taps_hbm, tap_own), (fg_hbm, fg), (sg_hbm, sg), (ct_hbm, ct), (vi_hbm, vi), (skip_hbm, skip_own))
        )
    ]
    for load in loads:
        load.start()

    tap_buf[0] = jnp.zeros((1, chunk), F32)
    slab[:, 0:half] = jnp.zeros((half, half), BF16)
    loads[0].wait()
    own = tap_own[...].astype(F32)
    tap_buf[me + 1] = jnp.concatenate([own[0:1], own[1:2]], axis=1)

    def messages(field):
        split = field.reshape(n, SUB, chunk)
        return jnp.concatenate([split[:, :, :half], split[:, :, half:]], axis=1).astype(BF16)

    plain = select_matrix(chunk, False)
    flipped = select_matrix(chunk, True)
    across = plain if channels == chunk else select_matrix(channels, False)
    loads[1].wait()
    loads[2].wait()
    gated = (fg[...].astype(F32) * sg[...].astype(F32)).astype(BF16)
    send1[0] = messages(lax.dot_general(across, gated, NT, preferred_element_type=F32))
    loads[3].wait()
    loads[4].wait()
    carried = (ct[...].astype(F32) * vi[...].astype(F32)).astype(BF16)
    carried = jnp.dot(flipped, carried, preferred_element_type=F32).astype(BF16)
    send1[1] = messages(lax.dot_general(across, carried, NT, preferred_element_type=F32))
    for way in range(2):
        recv1[way, me] = send1[way, me]

    lane = lax.broadcasted_iota(jnp.int32, (SUB, channels), 1)
    row = lax.broadcasted_iota(jnp.int32, (SUB, channels), 0)
    loads[5].wait()
    gains = jnp.sum(jnp.where(lane == me * SUB + row, skip_own[...], 0.0), axis=1, keepdims=True)

    pl.semaphore_wait(barrier, n - 1)

    def send_taps(peer):
        pltpu.make_async_remote_copy(
            src_ref=tap_buf.at[me + 1], dst_ref=tap_buf.at[me + 1],
            send_sem=tap_send, recv_sem=tap_recv.at[line], device_id={"seq": peer},
        ).start()

    def send_first(way, peer):
        pltpu.make_async_remote_copy(
            src_ref=send1.at[way, peer], dst_ref=recv1.at[way, me],
            send_sem=send1_sem.at[way], recv_sem=recv1_sem.at[way], device_id={"seq": peer},
        ).start()

    def send_second(way, peer):
        pltpu.make_async_remote_copy(
            src_ref=send2.at[way, peer], dst_ref=recv2.at[way, me],
            send_sem=send2_sem.at[way], recv_sem=recv2_sem.at[way], device_id={"seq": peer},
        ).start()

    def several(buf, count, send_sem, recv_sem):
        part = buf.at[pl.ds(0, count)]
        return pltpu.make_async_remote_copy(
            src_ref=part, dst_ref=part, send_sem=send_sem, recv_sem=recv_sem,
            device_id={"seq": lax.rem(me + 1, n)},
        )

    each_far_first(send_taps)
    for way in range(2):
        each_far_first(functools.partial(send_first, way))

    def build(j):
        window = jnp.concatenate([tap_buf[j][:, half:], tap_buf[j + 1]], axis=1)
        window = jnp.broadcast_to(window, (half, half + chunk))
        skewed = pltpu.roll(window, 0, 1, stride=1, stride_axis=0)
        slab[:, pl.ds(pl.multiple_of(j * chunk + half, half), chunk)] = skewed[:, half:].astype(BF16)

    for dx in sorted(range(LINES), key=lambda dx: (ring(dx, LINES), dx)):
        source = lax.rem(line + dx, LINES)
        arrived = size - 1 if dx == 0 else size
        if arrived:
            several(tap_buf, arrived, tap_send, tap_recv.at[source]).wait_recv()
        for place_of in range(1, size):
            build(source * size + place_of)
    for source in range(LINES):
        build(source * size)

    for way in range(2):
        first = several(recv1.at[way], n - 1, send1_sem.at[way], recv1_sem.at[way])
        first.wait_recv()

        def block_of(block):
            source, side = (block, 0) if block < n else (2 * n - 1 - block, 1)
            return recv1[way, source].astype(F32)[side * SUB:(side + 1) * SUB]

        for pair in range(0, n, 2):
            for side in range(2):
                lanes = slice(side * half, (side + 1) * half)
                both = jnp.concatenate([block_of(2 * pair + side), block_of(2 * pair + 2 + side)], axis=0)
                xbuf[pair * SUB:(pair + 2) * SUB, lanes] = both.astype(BF16)
                acc[pair * SUB:(pair + 1) * SUB, lanes] = gains * both[:SUB]
                acc[(pair + 1) * SUB:(pair + 2) * SUB, lanes] = gains * both[SUB:]

        total = n * SUB
        for d in range(n):
            top = slab[:, d * chunk + half:(d + 1) * chunk + half]
            low = slab[:, d * chunk:(d + 1) * chunk]
            lags = jnp.concatenate([top, low], axis=0)
            depth = total - d * SUB
            padded = -(-depth // (2 * SUB)) * 2 * SUB
            term = jnp.dot(xbuf[0:padded, :], lags, preferred_element_type=F32)
            acc[d * SUB:total, :] = acc[d * SUB:total, :] + term[:depth]

        for dst in range(n):
            pieces = [
                acc[(b // 2) * SUB:(b // 2 + 1) * SUB, (b % 2) * half:(b % 2 + 1) * half]
                for b in (dst, 2 * n - 1 - dst)
            ]
            send2[way, dst] = jnp.concatenate(pieces, axis=0).astype(BF16)
        each_corner_first(functools.partial(send_second, way))
        recv2[way, me] = send2[way, me]

    for way, (out, matrix) in enumerate(((fwd_ref, plain), (bwd_ref, flipped))):
        second = several(recv2.at[way], n - 1, send2_sem.at[way], recv2_sem.at[way])
        second.wait_recv()
        back = recv2[way].astype(F32)
        left = back[:, :SUB].reshape(channels, half)
        right = back[:, SUB:].reshape(channels, half)
        back = jnp.concatenate([left, right], axis=1).astype(BF16)
        out[...] = lax.dot_general(matrix, back, NT, preferred_element_type=F32).astype(BF16)

    several(tap_buf, n - 1, tap_send, tap_recv.at[0]).wait_send()
    for way in range(2):
        several(recv1.at[way], n - 1, send1_sem.at[way], recv1_sem.at[way]).wait_send()
        several(recv2.at[way], n - 1, send2_sem.at[way], recv2_sem.at[way]).wait_send()


def on_device(n, first_gate, second_gate, values_in, cotangent, filters, skip_gain):
    chunk, channels = first_gate.shape
    half = chunk // 2
    taps = filters.reshape(2, half)
    in_hbm = pl.BlockSpec(memory_space=pltpu.HBM)
    in_vmem = pl.BlockSpec(memory_space=pltpu.VMEM)
    result = pltpu.VMEM((chunk, channels), BF16)
    message = pltpu.VMEM((2, n, 2 * SUB, half), BF16)
    mixed_total, grad_mixed, first_gate, second_gate, values_in, cotangent = pl.pallas_call(
        functools.partial(kernel, n),
        out_shape=(result,) * 6,
        in_specs=[in_hbm] * 6,
        out_specs=(in_vmem,) * 6,
        scratch_shapes=[
            pltpu.VMEM((2, half), BF16),
            pltpu.VMEM((1, channels), F32),
            pltpu.VMEM((n + 1, 1, chunk), F32),
            message,
            message,
            pltpu.VMEM((n * SUB, chunk), BF16),
            pltpu.VMEM((half, half + n * chunk), BF16),
            pltpu.VMEM((n * SUB, chunk), F32),
            message,
            message,
            pltpu.SemaphoreType.DMA((6,)),
            pltpu.SemaphoreType.DMA,
            pltpu.SemaphoreType.DMA((LINES,)),
            pltpu.SemaphoreType.DMA((2,)),
            pltpu.SemaphoreType.DMA((2,)),
            pltpu.SemaphoreType.DMA((2,)),
            pltpu.SemaphoreType.DMA((2,)),
        ],
        compiler_params=pltpu.CompilerParams(
            collective_id=0, has_side_effects=True, vmem_limit_bytes=32 * 1024 * 1024
        ),
    )(*[
        pltpu.with_memory_space_constraint(x, pltpu.HBM)
        for x in (first_gate, second_gate, values_in, cotangent, taps, skip_gain.reshape(1, channels))
    ])
    mixed_total = mixed_total.astype(F32)
    grad_mixed = grad_mixed.astype(F32)
    output = (values_in.astype(F32) * mixed_total).astype(BF16)
    grad_first = (grad_mixed * second_gate.astype(F32)).astype(BF16)
    grad_second = (grad_mixed * first_gate.astype(F32)).astype(BF16)
    grad_values = (cotangent.astype(F32) * mixed_total).astype(BF16)
    return (output, grad_first, grad_second, grad_values)


def solution(mesh):
    rows = P("seq", "ch")
    return jax.shard_map(
        functools.partial(on_device, mesh.shape["seq"]),
        mesh=mesh,
        in_specs=(rows, rows, rows, rows, P(("ch", "seq")), P("ch")),
        out_specs=(rows, rows, rows, rows),
        check_vma=False,
    )
```

time: 30.2 us -> 27.3 us (0.904)
  the two profiles are of different devices: /device:TPU:2 before, /device:TPU:256 now
where the time goes in v3:
time: 27.3 us; the launch traced here: 27.1 us
  Pallas kernels  25.6 us (94%)
  other arithmetic  0.88 us (3%)
  between operations  0.64 us (2%)
    pallas_call x1, Pallas kernels, on_device(): pl.pallas_call(functools.partial(kernel, n), out_shape=(result,) * 6, in_...  25.6 us
    convert_element_type x1, other arithmetic, on_device(): grad_values = (cotangent.astype(F32) * mixed_total).astype(BF16)  0.88 us

profile of v3, /device:TPU:256, one launch (start us, length us, event | category | flops | bytes accessed | tf_op | source)
XLA Modules:
  0.0 27.1 jit_solution(2984013109556898032)
XLA Ops:
  0.6 25.6 %shard_map.93 = (bf16[256,256]{1,0:T(8,128)(2,1)S(1)}, bf16[256,256]{1,0:T(8,128)(2,1)S(1)}, bf16[256,256]{1,0:T(8,128)(2,1)S(1)}, bf16[256,256]{1,0:T(8,128)(2,...) custom-call(bf16[256,256]{1,0:T(8,128)(2,1)} %fg_hbm.1, bf16[256,256]{1,0:T(8,128)(2,1)} %sg_hbm.1, ...), custom_call_target="tpu_custom_call" | custom-call | tf_op jit(solution)/shard_map/pallas_call | solution.py:209
  26.3 0.9 %fusion.1 = (bf16[256,256]{1,0:T(8,128)(2,1)}, bf16[256,256]{1,0:T(8,128)(2,1)}, bf16[256,256]{1,0:T(8,128)(2,1)}, bf16[256,256]{1,0:T(8,128)(2,1)}) fusion(bf16[256,256]{1,0:T(8,128)(2,1)S(1)} %get-tuple-element.11, bf16[256,256]{1,0:T(8,128)(2,1)S(1)} %get-tuple-element.15, bf16[256,256]{1,0:T(8,128)(2,1)S(1)} %get-tuple-element.10, ...), kind=kLoop, calls=%fused_computation.5 | loop fusion | flops 917504 | bytes 1310720 | tf_op jit(solution)/shard_map/convert_element_type | solution.py:245

commit v4 on v3

--- a/solution.py
+++ b/solution.py
@@ -71,11 +71,10 @@
     for load in loads:
         load.start()
 
-    tap_buf[0] = jnp.zeros((1, chunk), F32)
+    tap_buf[0] = jnp.zeros((2, half), BF16)
     slab[:, 0:half] = jnp.zeros((half, half), BF16)
     loads[0].wait()
-    own = tap_own[...].astype(F32)
-    tap_buf[me + 1] = jnp.concatenate([own[0:1], own[1:2]], axis=1)
+    tap_buf[me + 1] = tap_own[...]
 
     def messages(field):
         split = field.reshape(n, SUB, chunk)
@@ -133,7 +132,8 @@
         each_far_first(functools.partial(send_first, way))
 
     def build(j):
-        window = jnp.concatenate([tap_buf[j][:, half:], tap_buf[j + 1]], axis=1)
+        before, here = tap_buf[j].astype(F32), tap_buf[j + 1].astype(F32)
+        window = jnp.concatenate([before[1:2], here[0:1], here[1:2]], axis=1)
         window = jnp.broadcast_to(window, (half, half + chunk))
         skewed = pltpu.roll(window, 0, 1, stride=1, stride_axis=0)
         slab[:, pl.ds(pl.multiple_of(j * chunk + half, half), chunk)] = skewed[:, half:].astype(BF16)
@@ -156,29 +156,29 @@
             source, side = (block, 0) if block < n else (2 * n - 1 - block, 1)
             return recv1[way, source].astype(F32)[side * SUB:(side + 1) * SUB]
 
-        for pair in range(0, n, 2):
-            for side in range(2):
-                lanes = slice(side * half, (side + 1) * half)
-                both = jnp.concatenate([block_of(2 * pair + side), block_of(2 * pair + 2 + side)], axis=0)
-                xbuf[pair * SUB:(pair + 2) * SUB, lanes] = both.astype(BF16)
-                acc[pair * SUB:(pair + 1) * SUB, lanes] = gains * both[:SUB]
-                acc[(pair + 1) * SUB:(pair + 2) * SUB, lanes] = gains * both[SUB:]
-
-        total = n * SUB
-        for d in range(n):
-            top = slab[:, d * chunk + half:(d + 1) * chunk + half]
-            low = slab[:, d * chunk:(d + 1) * chunk]
-            lags = jnp.concatenate([top, low], axis=0)
+        total = 2 * n * SUB
+        previous = jnp.zeros((SUB, half), F32)
+        for block in range(0, 2 * n, 2):
+            here, later = block_of(block), block_of(block + 1)
+            rows = slice(block * SUB, (block + 2) * SUB)
+            xbuf[rows, :half] = jnp.concatenate([previous, here], axis=0).astype(BF16)
+            xbuf[rows, half:] = jnp.concatenate([here, later], axis=0).astype(BF16)
+            acc[block * SUB:(block + 1) * SUB] = gains * here
+            acc[(block + 1) * SUB:(block + 2) * SUB] = gains * later
+            previous = later
+
+        for d in range(0, 2 * n, 4):
+            lag = [slab[:, (d + e + 1) * half:(d + e + 2) * half] for e in range(4)]
+            lags = jnp.concatenate(
+                [jnp.concatenate([lag[1], lag[3]], axis=1), jnp.concatenate([lag[0], lag[2]], axis=1)], axis=0
+            )
             depth = total - d * SUB
-            padded = -(-depth // (2 * SUB)) * 2 * SUB
-            term = jnp.dot(xbuf[0:padded, :], lags, preferred_element_type=F32)
-            acc[d * SUB:total, :] = acc[d * SUB:total, :] + term[:depth]
+            term = jnp.dot(xbuf[0:depth, :], lags, preferred_element_type=F32)
+            acc[d * SUB:total, :] = acc[d * SUB:total, :] + term[:, :half]
+            acc[(d + 2) * SUB:total, :] = acc[(d + 2) * SUB:total, :] + term[:depth - 2 * SUB, half:]
 
         for dst in range(n):
-            pieces = [
-                acc[(b // 2) * SUB:(b // 2 + 1) * SUB, (b % 2) * half:(b % 2 + 1) * half]
-                for b in (dst, 2 * n - 1 - dst)
-            ]
+            pieces = [acc[b * SUB:(b + 1) * SUB, :] for b in (dst, 2 * n - 1 - dst)]
             send2[way, dst] = jnp.concatenate(pieces, axis=0).astype(BF16)
         each_corner_first(functools.partial(send_second, way))
         recv2[way, me] = send2[way, me]
@@ -214,12 +214,12 @@
         scratch_shapes=[
             pltpu.VMEM((2, half), BF16),
             pltpu.VMEM((1, channels), F32),
-            pltpu.VMEM((n + 1, 1, chunk), F32),
-            message,
-            message,
-            pltpu.VMEM((n * SUB, chunk), BF16),
+            pltpu.VMEM((n + 1, 2, half), BF16),
+            message,
+            message,
+            pltpu.VMEM((2 * n * SUB, chunk), BF16),
             pltpu.VMEM((half, half + n * chunk), BF16),
-            pltpu.VMEM((n * SUB, chunk), F32),
+            pltpu.VMEM((2 * n * SUB, half), F32),
             message,
             message,
             pltpu.SemaphoreType.DMA((6,)),

time: 27.3 us -> 26.8 us (0.982)
  the two profiles are of different devices: /device:TPU:256 before, /device:TPU:144 now
where the time goes in v4:
time: 26.8 us; the launch traced here: 26.6 us
  Pallas kernels  25.1 us (94%)
  other arithmetic  0.88 us (3%)
  between operations  0.64 us (2%)
    pallas_call x1, Pallas kernels, on_device(): pl.pallas_call(functools.partial(kernel, n), out_shape=(result,) * 6, in_...  25.1 us
    convert_element_type x1, other arithmetic, on_device(): grad_values = (cotangent.astype(F32) * mixed_total).astype(BF16)  0.88 us

profile of v4, /device:TPU:144, one launch (start us, length us, event | category | flops | bytes accessed | tf_op | source)
XLA Modules:
  0.0 26.6 jit_solution(4108212581362432143)
XLA Ops:
  0.6 25.1 %shard_map.93 = (bf16[256,256]{1,0:T(8,128)(2,1)S(1)}, bf16[256,256]{1,0:T(8,128)(2,1)S(1)}, bf16[256,256]{1,0:T(8,128)(2,1)S(1)}, bf16[256,256]{1,0:T(8,128)(2,...) custom-call(bf16[256,256]{1,0:T(8,128)(2,1)} %fg_hbm.1, bf16[256,256]{1,0:T(8,128)(2,1)} %sg_hbm.1, ...), custom_call_target="tpu_custom_call" | custom-call | tf_op jit(solution)/shard_map/pallas_call | solution.py:209
  25.7 0.9 %fusion.1 = (bf16[256,256]{1,0:T(8,128)(2,1)}, bf16[256,256]{1,0:T(8,128)(2,1)}, bf16[256,256]{1,0:T(8,128)(2,1)}, bf16[256,256]{1,0:T(8,128)(2,1)}) fusion(bf16[256,256]{1,0:T(8,128)(2,1)S(1)} %get-tuple-element.11, bf16[256,256]{1,0:T(8,128)(2,1)S(1)} %get-tuple-element.15, bf16[256,256]{1,0:T(8,128)(2,1)S(1)} %get-tuple-element.10, ...), kind=kLoop, calls=%fused_computation.5 | loop fusion | flops 917504 | bytes 1310720 | tf_op jit(solution)/shard_map/convert_element_type | solution.py:245

commit v5 on v4

--- a/solution.py
+++ b/solution.py
@@ -36,11 +36,35 @@
     return sorted(range(n), key=lambda d: (ring(d % size, size) * 2 + ring(d // size, LINES) * 2 + (d % size > size // 2), d))
 
 
+def rows_of(messages):
+    n, _, half = messages.shape
+    back = messages[...].astype(F32)
+    left = back[:, :SUB].reshape(n * SUB, half)
+    right = back[:, SUB:].reshape(n * SUB, half)
+    return jnp.concatenate([left, right], axis=1).astype(BF16)
+
+
+def finish(mixed_ref, back_ref, fg, sg, vi, ct, out, grad_first, grad_second, grad_values, result, sem):
+    def put(k, value, target):
+        result[k] = value.astype(BF16)
+        copy = pltpu.make_async_copy(result.at[k], target, sem.at[k])
+        copy.start()
+        return copy
+
+    mixed = mixed_ref[...].astype(F32)
+    copies = [put(0, vi[...].astype(F32) * mixed, out), put(3, ct[...].astype(F32) * mixed, grad_values)]
+    flipped = select_matrix(fg.shape[0], True)
+    grad = lax.dot_general(flipped, rows_of(back_ref), NT, preferred_element_type=F32)
+    copies += [put(1, grad * sg[...].astype(F32), grad_first), put(2, grad * fg[...].astype(F32), grad_second)]
+    for copy in copies:
+        copy.wait()
+
+
 def kernel(
     n,
     fg_hbm, sg_hbm, vi_hbm, ct_hbm, taps_hbm, skip_hbm,
-    fwd_ref, bwd_ref, fg, sg, vi, ct,
-    tap_own, skip_own, tap_buf, send1, recv1, xbuf, slab, acc, send2, recv2,
+    fwd_ref, recv2_bwd, fg, sg, vi, ct,
+    tap_own, skip_own, tap_buf, send1, recv1, xbuf, slab, acc, send2, recv2_fwd,
     in_sem, tap_send, tap_recv, send1_sem, recv1_sem, send2_sem, recv2_sem,
 ):
     me = lax.axis_index("seq")
@@ -114,9 +138,11 @@
             send_sem=send1_sem.at[way], recv_sem=recv1_sem.at[way], device_id={"seq": peer},
         ).start()
 
+    recv2 = (recv2_fwd, recv2_bwd)
+
     def send_second(way, peer):
         pltpu.make_async_remote_copy(
-            src_ref=send2.at[way, peer], dst_ref=recv2.at[way, me],
+            src_ref=send2.at[way, peer], dst_ref=recv2[way].at[me],
             send_sem=send2_sem.at[way], recv_sem=recv2_sem.at[way], device_id={"seq": peer},
         ).start()
 
@@ -181,21 +207,16 @@
             pieces = [acc[b * SUB:(b + 1) * SUB, :] for b in (dst, 2 * n - 1 - dst)]
             send2[way, dst] = jnp.concatenate(pieces, axis=0).astype(BF16)
         each_corner_first(functools.partial(send_second, way))
-        recv2[way, me] = send2[way, me]
-
-    for way, (out, matrix) in enumerate(((fwd_ref, plain), (bwd_ref, flipped))):
-        second = several(recv2.at[way], n - 1, send2_sem.at[way], recv2_sem.at[way])
-        second.wait_recv()
-        back = recv2[way].astype(F32)
-        left = back[:, :SUB].reshape(channels, half)
-        right = back[:, SUB:].reshape(channels, half)
-        back = jnp.concatenate([left, right], axis=1).astype(BF16)
-        out[...] = lax.dot_general(matrix, back, NT, preferred_element_type=F32).astype(BF16)
+        recv2[way][me] = send2[way, me]
+
+    several(recv2_fwd, n - 1, send2_sem.at[0], recv2_sem.at[0]).wait_recv()
+    fwd_ref[...] = lax.dot_general(plain, rows_of(recv2_fwd), NT, preferred_element_type=F32).astype(BF16)
+    several(recv2_bwd, n - 1, send2_sem.at[1], recv2_sem.at[1]).wait_recv()
 
     several(tap_buf, n - 1, tap_send, tap_recv.at[0]).wait_send()
     for way in range(2):
         several(recv1.at[way], n - 1, send1_sem.at[way], recv1_sem.at[way]).wait_send()
-        several(recv2.at[way], n - 1, send2_sem.at[way], recv2_sem.at[way]).wait_send()
+        several(recv2[way], n - 1, send2_sem.at[way], recv2_sem.at[way]).wait_send()
 
 
 def on_device(n, first_gate, second_gate, values_in, cotangent, filters, skip_gain):
@@ -206,9 +227,9 @@
     in_vmem = pl.BlockSpec(memory_space=pltpu.VMEM)
     result = pltpu.VMEM((chunk, channels), BF16)
     message = pltpu.VMEM((2, n, 2 * SUB, half), BF16)
-    mixed_total, grad_mixed, first_gate, second_gate, values_in, cotangent = pl.pallas_call(
+    mixed, back, *gates = pl.pallas_call(
         functools.partial(kernel, n),
-        out_shape=(result,) * 6,
+        out_shape=(result, pltpu.VMEM((n, 2 * SUB, half), BF16)) + (result,) * 4,
         in_specs=[in_hbm] * 6,
         out_specs=(in_vmem,) * 6,
         scratch_shapes=[
@@ -221,7 +242,7 @@
             pltpu.VMEM((half, half + n * chunk), BF16),
             pltpu.VMEM((2 * n * SUB, half), F32),
             message,
-            message,
+            pltpu.VMEM((n, 2 * SUB, half), BF16),
             pltpu.SemaphoreType.DMA((6,)),
             pltpu.SemaphoreType.DMA,
             pltpu.SemaphoreType.DMA((LINES,)),
@@ -237,13 +258,14 @@
         pltpu.with_memory_space_constraint(x, pltpu.HBM)
         for x in (first_gate, second_gate, values_in, cotangent, taps, skip_gain.reshape(1, channels))
     ])
-    mixed_total = mixed_total.astype(F32)
-    grad_mixed = grad_mixed.astype(F32)
-    output = (values_in.astype(F32) * mixed_total).astype(BF16)
-    grad_first = (grad_mixed * second_gate.astype(F32)).astype(BF16)
-    grad_second = (grad_mixed * first_gate.astype(F32)).astype(BF16)
-    grad_values = (cotangent.astype(F32) * mixed_total).astype(BF16)
-    return (output, grad_first, grad_second, grad_values)
+    return pl.pallas_call(
+        finish,
+        out_shape=(jax.ShapeDtypeStruct((chunk, channels), BF16),) * 4,
+        in_specs=[in_vmem] * 6,
+        out_specs=(in_hbm,) * 4,
+        scratch_shapes=[pltpu.VMEM((4, chunk, channels), BF16), pltpu.SemaphoreType.DMA((4,))],
+        compiler_params=pltpu.CompilerParams(vmem_limit_bytes=16 * 1024 * 1024),
+    )(*[pltpu.with_memory_space_constraint(x, pltpu.VMEM) for x in (mixed, back, *gates)])
 
 
 def solution(mesh):

time: 26.8 us -> 26.6 us (level)
  the two profiles are of different devices: /device:TPU:144 before, /device:TPU:464 now
where the time goes in v5:
time: 26.6 us; the launch traced here: 26.5 us
  Pallas kernels  25.8 us (97%)
  between operations  0.64 us (2%)
    pallas_call x1, Pallas kernels, on_device(): pl.pallas_call(functools.partial(kernel, n), out_shape=(result, pltpu.VME...  24.9 us
    pallas_call x1, Pallas kernels, on_device(): pl.pallas_call(finish, out_shape=(jax.ShapeDtypeStruct((chunk, channels),...  0.97 us

profile of v5, /device:TPU:464, one launch (start us, length us, event | category | flops | bytes accessed | tf_op | source)
XLA Modules:
  0.0 26.5 jit_solution(10445616567471621242)
XLA Ops:
  0.6 24.9 %shard_map.93 = (bf16[256,256]{1,0:T(8,128)(2,1)S(1)}, bf16[32,16,128]{2,1,0:T(8,128)(2,1)S(1)}, bf16[256,256]{1,0:T(8,128)(2,1)S(1)}, bf16[256,256]{1,0:T(8,128...) custom-call(bf16[256,256]{1,0:T(8,128)(2,1)} %fg_hbm.1, bf16[256,256]{1,0:T(8,128)(2,1)} %sg_hbm.1, ...), custom_call_target="tpu_custom_call" | custom-call | tf_op jit(solution)/shard_map/pallas_call | solution.py:230
  25.5 1.0 %shard_map.94 = (bf16[256,256]{1,0:T(8,128)(2,1)}, bf16[256,256]{1,0:T(8,128)(2,1)}, bf16[256,256]{1,0:T(8,128)(2,1)}, bf16[256,256]{1,0:T(8,128)(2,1)}) custom-call(bf16[256,256]{1,0:T(8,128)(2,1)S(1)} %get-tuple-element.10.mixed_ref, bf16[32,16,128]{2,1,0:T(8,128)(2,1)S(1)} %get-tuple-element.11.back_ref, bf16[256,256]{1,0:T(8,128)(2,1)S(1)} %get-tuple-element.12.fg, ...), custom_call_target="tpu_custom_call" | custom-call | tf_op jit(solution)/shard_map/pallas_call | solution.py:261

commit v6 on v5

--- a/solution.py
+++ b/solution.py
@@ -44,7 +44,7 @@
     return jnp.concatenate([left, right], axis=1).astype(BF16)
 
 
-def finish(mixed_ref, back_ref, fg, sg, vi, ct, out, grad_first, grad_second, grad_values, result, sem):
+def finish(mixed_ref, back_ref, flip, fg, sg, vi, ct, out, grad_first, grad_second, grad_values, result, sem):
     def put(k, value, target):
         result[k] = value.astype(BF16)
         copy = pltpu.make_async_copy(result.at[k], target, sem.at[k])
@@ -53,8 +53,7 @@
 
     mixed = mixed_ref[...].astype(F32)
     copies = [put(0, vi[...].astype(F32) * mixed, out), put(3, ct[...].astype(F32) * mixed, grad_values)]
-    flipped = select_matrix(fg.shape[0], True)
-    grad = lax.dot_general(flipped, rows_of(back_ref), NT, preferred_element_type=F32)
+    grad = lax.dot_general(flip[...], rows_of(back_ref), NT, preferred_element_type=F32)
     copies += [put(1, grad * sg[...].astype(F32), grad_first), put(2, grad * fg[...].astype(F32), grad_second)]
     for copy in copies:
         copy.wait()
@@ -63,7 +62,7 @@
 def kernel(
     n,
     fg_hbm, sg_hbm, vi_hbm, ct_hbm, taps_hbm, skip_hbm,
-    fwd_ref, recv2_bwd, fg, sg, vi, ct,
+    fwd_ref, recv2_bwd, flip, fg, sg, vi, ct,
     tap_own, skip_own, tap_buf, send1, recv1, xbuf, slab, acc, send2, recv2_fwd,
     in_sem, tap_send, tap_recv, send1_sem, recv1_sem, send2_sem, recv2_sem,
 ):
@@ -106,6 +105,7 @@
 
     plain = select_matrix(chunk, False)
     flipped = select_matrix(chunk, True)
+    flip[...] = flipped
     across = plain if channels == chunk else select_matrix(channels, False)
     loads[1].wait()
     loads[2].wait()
@@ -153,9 +153,13 @@
             device_id={"seq": lax.rem(me + 1, n)},
         )
 
+    patient = lax.rem(lax.axis_index("ch"), 2) == 1
     each_far_first(send_taps)
-    for way in range(2):
-        each_far_first(functools.partial(send_first, way))
+    each_far_first(functools.partial(send_first, 0))
+
+    @pl.when(jnp.logical_not(patient))
+    def _():
+        each_far_first(functools.partial(send_first, 1))
 
     def build(j):
         before, here = tap_buf[j].astype(F32), tap_buf[j + 1].astype(F32)
@@ -164,15 +168,23 @@
         skewed = pltpu.roll(window, 0, 1, stride=1, stride_axis=0)
         slab[:, pl.ds(pl.multiple_of(j * chunk + half, half), chunk)] = skewed[:, half:].astype(BF16)
 
+    here = []
     for dx in sorted(range(LINES), key=lambda dx: (ring(dx, LINES), dx)):
         source = lax.rem(line + dx, LINES)
         arrived = size - 1 if dx == 0 else size
         if arrived:
             several(tap_buf, arrived, tap_send, tap_recv.at[source]).wait_recv()
+        here.append(dx)
         for place_of in range(1, size):
             build(source * size + place_of)
-    for source in range(LINES):
-        build(source * size)
+        if len(here) == 2:
+            @pl.when(patient)
+            def _():
+                each_far_first(functools.partial(send_first, 1))
+
+        for first in (dx, (dx + 1) % LINES):
+            if first in here and (first - 1) % LINES in here:
+                build(lax.rem(line + first, LINES) * size)
 
     for way in range(2):
         first = several(recv1.at[way], n - 1, send1_sem.at[way], recv1_sem.at[way])
@@ -227,11 +239,11 @@
     in_vmem = pl.BlockSpec(memory_space=pltpu.VMEM)
     result = pltpu.VMEM((chunk, channels), BF16)
     message = pltpu.VMEM((2, n, 2 * SUB, half), BF16)
-    mixed, back, *gates = pl.pallas_call(
+    mixed, back, flip, *gates = pl.pallas_call(
         functools.partial(kernel, n),
-        out_shape=(result, pltpu.VMEM((n, 2 * SUB, half), BF16)) + (result,) * 4,
+        out_shape=(result, pltpu.VMEM((n, 2 * SUB, half), BF16), pltpu.VMEM((chunk, chunk), BF16)) + (result,) * 4,
         in_specs=[in_hbm] * 6,
-        out_specs=(in_vmem,) * 6,
+        out_specs=(in_vmem,) * 7,
         scratch_shapes=[
             pltpu.VMEM((2, half), BF16),
             pltpu.VMEM((1, channels), F32),
@@ -261,11 +273,11 @@
     return pl.pallas_call(
         finish,
         out_shape=(jax.ShapeDtypeStruct((chunk, channels), BF16),) * 4,
-        in_specs=[in_vmem] * 6,
+        in_specs=[in_vmem] * 7,
         out_specs=(in_hbm,) * 4,
         scratch_shapes=[pltpu.VMEM((4, chunk, channels), BF16), pltpu.SemaphoreType.DMA((4,))],
         compiler_params=pltpu.CompilerParams(vmem_limit_bytes=16 * 1024 * 1024),
-    )(*[pltpu.with_memory_space_constraint(x, pltpu.VMEM) for x in (mixed, back, *gates)])
+    )(*[pltpu.with_memory_space_constraint(x, pltpu.VMEM) for x in (mixed, back, flip, *gates)])
 
 
 def solution(mesh):

time: 26.6 us -> 26.5 us (level)
  the two profiles are of different devices: /device:TPU:464 before, /device:TPU:18 now
where the time goes in v6:
time: 26.5 us; the launch traced here: 26.4 us
  Pallas kernels  25.8 us (97%)
  between operations  0.64 us (2%)
    pallas_call x1, Pallas kernels, on_device(): pl.pallas_call(functools.partial(kernel, n), out_shape=(result, pltpu.VME...  24.8 us
    pallas_call x1, Pallas kernels, on_device(): pl.pallas_call(finish, out_shape=(jax.ShapeDtypeStruct((chunk, channels),...  0.97 us

profile of v6, /device:TPU:18, one launch (start us, length us, event | category | flops | bytes accessed | tf_op | source)
XLA Modules:
  0.0 26.4 jit_solution(8881059339271144774)
XLA Ops:
  0.6 24.8 %shard_map.93 = (bf16[256,256]{1,0:T(8,128)(2,1)S(1)}, bf16[32,16,128]{2,1,0:T(8,128)(2,1)S(1)}, bf16[256,256]{1,0:T(8,128)(2,1)S(1)}, bf16[256,256]{1,0:T(8,128...) custom-call(bf16[256,256]{1,0:T(8,128)(2,1)} %fg_hbm.1, ...), custom_call_target="tpu_custom_call" | custom-call | tf_op jit(solution)/shard_map/pallas_call | solution.py:242
  25.4 1.0 %shard_map.94 = (bf16[256,256]{1,0:T(8,128)(2,1)}, bf16[256,256]{1,0:T(8,128)(2,1)}, bf16[256,256]{1,0:T(8,128)(2,1)}, bf16[256,256]{1,0:T(8,128)(2,1)}) custom-call(bf16[256,256]{1,0:T(8,128)(2,1)S(1)} %get-tuple-element.11.mixed_ref, bf16[32,16,128]{2,1,0:T(8,128)(2,1)S(1)} %get-tuple-element.12.back_ref, bf16[256,256]{1,0:T(8,128)(2,1)S(1)} %get-tuple-element.13.flip, ...), custom_call_target="tpu_custom_call" | custom-call | tf_op jit(solution)/shard_map/pallas_call | solution.py:273

commit v7 on v6

--- a/solution.py
+++ b/solution.py
@@ -28,7 +28,7 @@
 def far_first(n):
     size = n // LINES
     steps = [(dx, dy) for dx in range(LINES) for dy in range(size)][1:]
-    return sorted(steps, key=lambda s: (-ring(s[1], size), -ring(s[0], LINES), s))
+    return sorted(steps, key=lambda s: (-ring(s[1], size) - ring(s[0], LINES), s))
 
 
 def corner_first(n):

time: 26.5 us -> 26.6 us (level)
  the two profiles are of different devices: /device:TPU:18 before, /device:TPU:2 now
where the time goes in v7:
time: 26.6 us; the launch traced here: 26.4 us
  Pallas kernels  25.8 us (97%)
  between operations  0.64 us (2%)
    pallas_call x1, Pallas kernels, on_device(): pl.pallas_call(functools.partial(kernel, n), out_shape=(result, pltpu.VME...  24.8 us
    pallas_call x1, Pallas kernels, on_device(): pl.pallas_call(finish, out_shape=(jax.ShapeDtypeStruct((chunk, channels),...  0.97 us

profile of v7, /device:TPU:2, one launch (start us, length us, event | category | flops | bytes accessed | tf_op | source)
XLA Modules:
  0.0 26.4 jit_solution(6004552418182370725)
XLA Ops:
  0.6 24.8 %shard_map.93 = (bf16[256,256]{1,0:T(8,128)(2,1)S(1)}, bf16[32,16,128]{2,1,0:T(8,128)(2,1)S(1)}, bf16[256,256]{1,0:T(8,128)(2,1)S(1)}, bf16[256,256]{1,0:T(8,128...) custom-call(bf16[256,256]{1,0:T(8,128)(2,1)} %fg_hbm.1, ...), custom_call_target="tpu_custom_call" | custom-call | tf_op jit(solution)/shard_map/pallas_call | solution.py:242
  25.5 1.0 %shard_map.94 = (bf16[256,256]{1,0:T(8,128)(2,1)}, bf16[256,256]{1,0:T(8,128)(2,1)}, bf16[256,256]{1,0:T(8,128)(2,1)}, bf16[256,256]{1,0:T(8,128)(2,1)}) custom-call(bf16[256,256]{1,0:T(8,128)(2,1)S(1)} %get-tuple-element.11.mixed_ref, bf16[32,16,128]{2,1,0:T(8,128)(2,1)S(1)} %get-tuple-element.12.back_ref, bf16[256,256]{1,0:T(8,128)(2,1)S(1)} %get-tuple-element.13.flip, ...), custom_call_target="tpu_custom_call" | custom-call | tf_op jit(solution)/shard_map/pallas_call | solution.py:273
